TPU v7x, 1024 devices: a whole 4x8x16 slice. The times are simulated.
1024 devices in a mesh: row: 16 (over y, x_lo), col: 64 (over z, x_hi, core).
Axes of the slice: x: 4 (x_hi: 2, x_lo: 2; x = x_hi * 2 + x_lo), y: 8, z: 16, core: 2. Of those that a mesh axis runs over, the one named last changes fastest.
Arguments:
- normed: bfloat16 [1024, 6144], P('col', 'row'), may hold values from -6 to 6
- upstream: bfloat16 [1024, 6144], P('col', 'row'), may hold values from -6 to 6
- loss_weight: float32 [1024], P('col'), may hold values from 0.05 to 0.5
- w_in: bfloat16 [6144, 24576], P('row', 'col'), may hold values from -0.078125 to 0.078125
- b_in: float32 [24576], P('col'), may hold values from -3 to 3
- w_out: bfloat16 [24576, 6144], P('col', 'row'), may hold values from -0.0390625 to 0.0390625
Outputs:
- grad_normed: bfloat16 [1024, 6144], P('col', 'row')
- grad_w_in: float32 [6144, 24576], P('row', 'col')
- grad_b_in: float32 [24576], P('col')
- grad_w_out: float32 [24576, 6144], P('col', 'row')
All inputs are finite; a program needn't handle non-finite values.
Results may differ from a plain program's by a relative error of at most 0.028.
Values may be sent and summed in bfloat16 or wider, within the bound.
A program may use at most 32 MiB of HBM per device.

v0:
```python
import jax
import jax.numpy as jnp
from jax import lax
from jax.sharding import PartitionSpec as P


def gelu_exact(values):
    return jax.nn.gelu(values, approximate=False)


def on_device(normed, upstream, loss_weight, w_in, b_in, w_out):
    weighted = (upstream.astype(jnp.float32) * loss_weight[:, None]).astype(jnp.bfloat16)
    h_all, g_all = (
        lax.all_gather(normed, "col", axis=0, tiled=True),
        lax.all_gather(weighted, "col", axis=0, tiled=True),
    )
    part_pre = jnp.dot(h_all, w_in, preferred_element_type=jnp.float32)
    part_grad = lax.dot_general(
        g_all, w_out, (((1,), (1,)), ((), ())), preferred_element_type=jnp.float32
    )
    pre_local, grad_local = (
        lax.psum_scatter(
            part_pre.astype(jnp.bfloat16), "row", scatter_dimension=0, tiled=True
        ).astype(jnp.float32),
        lax.psum_scatter(
            part_grad.astype(jnp.bfloat16), "row", scatter_dimension=0, tiled=True
        ).astype(jnp.float32),
    )
    activated, pullback = jax.vjp(gelu_exact, pre_local + b_in[None, :])
    grad_pre = pullback(grad_local)[0].astype(jnp.bfloat16)
    act_all, pre_grad_all = (
        lax.all_gather(activated.astype(jnp.bfloat16), "row", axis=0, tiled=True),
        lax.all_gather(grad_pre, "row", axis=0, tiled=True),
    )
    grad_w_out = lax.dot_general(
        act_all, g_all, (((0,), (0,)), ((), ())), preferred_element_type=jnp.float32
    )
    grad_w_in = lax.dot_general(
        h_all, pre_grad_all, (((0,), (0,)), ((), ())), preferred_element_type=jnp.float32
    )
    grad_b_in = jnp.sum(pre_grad_all.astype(jnp.float32), axis=0)
    grad_normed = lax.psum_scatter(
        lax.dot_general(
            pre_grad_all, w_in, (((1,), (1,)), ((), ())), preferred_element_type=jnp.float32
        ),
        "col",
        scatter_dimension=0,
        tiled=True,
    )
    return (grad_normed.astype(jnp.bfloat16), grad_w_in, grad_b_in, grad_w_out)


def solution(mesh):
    placed = (
        P("col", "row"),
        P("col", "row"),
        P("col"),
        P("row", "col"),
        P("col"),
        P("col", "row"),
    )
    return jax.shard_map(
        on_device,
        mesh=mesh,
        in_specs=placed,
        out_specs=(P("col", "row"), P("row", "col"), P("col"), P("col", "row")),
        check_vma=False,
    )
```

profile of v0, /device:TPU:16, one launch (start us, length us, event | category | flops | bytes accessed | tf_op | source)
XLA Modules:
  0.0 521.9 jit_solution(17609894207547694361)
XLA Ops:
  7.2 0.0 copy-start
  7.2 0.0 copy-start.4
  7.2 0.0 copy-start.2
  7.2 0.0 reduce-scatter.4.cloned.1.call-start
  7.2 92.6 %all_gather.12 = bf16[1024,384]{1,0:T(8,128)(2,1)S(1)} all-gather(bf16[16,384]{1,0:T(8,128)(2,1)} %param.6), channel_id=1, replica_groups=mesh['row'=16,'col'=64] {'col'}, dimensions={0}, use_global_device_ids=true | all-gather | bytes 798720 | tf_op jit(solution)/shard_map/all_gather | solution.py:14
  99.8 0.0 copy-done
  99.8 0.0 copy-start.1
  99.8 1.5 convolution_convert_fusion.1
  101.4 0.0 reduce-scatter.4.cloned.1.call-update
  101.4 0.0 reduce-scatter.6.cloned.1.call-start
  101.4 0.0 copy-done.4
  101.4 0.0 copy-done.2
  101.4 0.1 multiply_convert_fusion.1
  101.5 0.0 copy-start.3
  101.5 74.0 %all_gather.13 = bf16[1024,384]{1,0:T(8,128)(2,1)S(1)} all-gather(bf16[16,384]{1,0:T(8,128)(2,1)S(1)} %multiply_convert_fusion.1), channel_id=1, replica_groups=mesh['row'=16,'col'=64] {'col'}, dimensions={0}, use_global_device_ids=true | all-gather | bytes 798720 | tf_op jit(solution)/shard_map/all_gather | solution.py:15
  175.5 0.0 copy-done.1
  175.6 1.5 convolution_convert_fusion
  177.1 0.0 reduce-scatter.6.cloned.1.call-update
  177.1 0.0 reduce-scatter.8.cloned.1.call-start
  177.2 0.0 reduce-scatter.4.cloned.1.call-done
  177.2 0.0 copy-done.3
  177.2 1.0 multiply_convert_fusion
  178.2 70.5 %reduce-scatter.6.cloned.1.call-done = bf16[64,384]{1,0:T(8,128)(2,1)} async-done(((bf16[1024,384]{1,0:T(8,128)(2,1)}), bf16[64,384]{1,0:T(8,128)(2,1)}) %reduce-scatter.6.cloned.1.call-update) | async-done | bytes 49168 | tf_op jit(solution)/shard_map/reduce_scatter | solution.py:25
  248.8 0.9 fusion.5
  249.7 36.2 %all_gather.14 = bf16[1024,384]{1,0:T(8,128)(2,1)S(1)} all-gather(bf16[64,384]{1,0:T(8,128)(2,1)S(1)} %fusion.5), channel_id=1, replica_groups=mesh['row'=16,'col'=64] {'row'}, dimensions={0}, use_global_device_ids=true | all-gather | bytes 835584 | tf_op jit(solution)/shard_map/all_gather | solution.py:33
  285.9 1.8 fusion.20
  287.7 0.0 reduce-scatter.8.cloned.1.call-update
  287.7 0.6 convolution_bitcast_fusion
  288.3 1.1 copy.10
  289.4 0.7 convert_reduce_fusion
  290.1 33.9 %all_gather.15 = bf16[1024,384]{1,0:T(8,128)(2,1)S(1)} all-gather(bf16[64,384]{1,0:T(8,128)(2,1)S(1)} %get-tuple-element.8), channel_id=1, replica_groups=mesh['row'=16,'col'=64] {'row'}, dimensions={0}, use_global_device_ids=true | all-gather | bytes 835584 | tf_op jit(solution)/shard_map/all_gather | solution.py:32
  324.0 1.4 fusion.21
  325.4 188.6 %reduce-scatter.8.cloned.1.call-done = f32[16,384]{1,0:T(8,128)} async-done(((f32[1024,384]{1,0:T(8,128)}), f32[16,384]{1,0:T(8,128)}) %reduce-scatter.8.cloned.1.call-update) | async-done | bytes 24592 | tf_op jit(solution)/shard_map/reduce_scatter | solution.py:42
  514.0 1.3 convert_element_type.37
Async XLA Ops:
  7.2 92.7 %copy-start = (bf16[384,384]{1,0:T(8,128)(2,1)S(1)}, bf16[384,384]{1,0:T(8,128)(2,1)}, u32[]{:S(2)}) copy-start(bf16[384,384]{1,0:T(8,128)(2,1)} %param.9) | copy-start | bytes 884740
  7.2 94.2 %copy-start.4 = (f32[16]{0:T(128)S(1)}, f32[16]{0:T(128)}, u32[]{:S(2)}) copy-start(f32[16]{0:T(128)} %param.8) | copy-start | bytes 196
  7.2 94.2 %copy-start.2 = (bf16[16,384]{1,0:T(8,128)(2,1)S(1)}, bf16[16,384]{1,0:T(8,128)(2,1)}, u32[]{:S(2)}) copy-start(bf16[16,384]{1,0:T(8,128)(2,1)} %param.7) | copy-start | bytes 36868
  7.2 170.0 %reduce-scatter.4.cloned.1.call-start = ((), (), s32[]{:S(2)}) async-start(), calls=%async_computation.3 | async-start | bytes 835584 | tf_op jit(solution)/shard_map/reduce_scatter | solution.py:22
  99.8 75.7 %copy-start.1 = (bf16[384,384]{1,0:T(8,128)(2,1)S(1)}, bf16[384,384]{1,0:T(8,128)(2,1)}, u32[]{:S(2)}) copy-start(bf16[384,384]{1,0:T(8,128)(2,1)} %param.11) | copy-start | bytes 884740
  101.4 147.4 %reduce-scatter.6.cloned.1.call-start = ((), (), s32[]{:S(2)}) async-start(), calls=%async_computation.4 | async-start | bytes 835584 | tf_op jit(solution)/shard_map/reduce_scatter | solution.py:25
  101.5 75.7 %copy-start.3 = (f32[384]{0:T(512)S(1)}, f32[384]{0:T(512)}, u32[]{:S(2)}) copy-start(f32[384]{0:T(512)} %param.10) | copy-start | bytes 4612
  177.1 336.9 %reduce-scatter.8.cloned.1.call-start = ((), (), s32[]{:S(2)}) async-start(), calls=%async_computation.5 | async-start | bytes 1597440 | tf_op jit(solution)/shard_map/reduce_scatter | solution.py:42
Sparse Core Ops, SparseCore 0:
  101.5 65.3 reduce-scatter.3
  177.2 71.4 reduce-scatter.5
  287.8 226.1 reduce-scatter.7
where the time goes:
time: 522 us
  waiting for transfers between devices  259 us (50%)
  blocking collectives  237 us (45%)
  between operations  13.8 us (3%)
  matrix products  6.88 us (1%)
    reduce_scatter x1, waiting for transfers between devices, on_device(): lax.psum_scatter(lax.dot_general(pre_grad_all, w_in, (((1,), (1,)), ((),...  189 us
    all_gather x1, blocking collectives, on_device(): lax.all_gather(normed, 'col', axis=0, tiled=True)  92.6 us
    all_gather x1, blocking collectives, on_device(): lax.all_gather(weighted, 'col', axis=0, tiled=True)  74 us
    reduce_scatter x1, waiting for transfers between devices, on_device(): lax.psum_scatter(part_grad.astype(jnp.bfloat16), 'row', scatter_dimension...  70.5 us
    all_gather x1, blocking collectives, on_device(): lax.all_gather(grad_pre, 'row', axis=0, tiled=True)  36.2 us
    all_gather x1, blocking collectives, on_device(): lax.all_gather(activated.astype(jnp.bfloat16), 'row', axis=0, tiled=True)  33.9 us
  transfers between devices with their start and end apart: 3, of which 2 were waited for; matrix products, arithmetic and copies ran while one was open for 1% of the time, Pallas kernels for 0%

commit v1 on v0

v1 whole, which is shorter than its diff:
```python
import functools
import math

import jax
import jax.numpy as jnp
from jax import lax
from jax.experimental import pallas as pl
from jax.experimental.pallas import tpu as pltpu
from jax.sharding import PartitionSpec as P

BF16 = jnp.bfloat16
F32 = jnp.float32


def copy_keys(ny, nz):
    chunks, half = nz // ny, ny // 2
    keys = [("az", s) for s in range(nz) if s != nz // 2]
    keys += [(kind, s) for kind in ("ax", "as") for s in range(nz)]
    for kind in ("c", "e"):
        for k in range(chunks):
            for way in (0, 1):
                for d in range(half, 0, -1):
                    keys += [(kind, k, way, d, j) for j in (0, 1) if d < half or j == way]
            keys.append((kind + "x", k))
    keys += [("gs", k, i) for k in range(chunks) for i in (0, 1)]
    keys += [("gz", s) for s in range(nz) if s != nz // 2]
    keys.append(("gx",))
    return {key: i for i, key in enumerate(keys)}


def kernel(ny, nz, blk, f, normed, upstream, loss_weight, w_in, b_in, w_out,
           o_normed, o_w_in, o_b_in, o_w_out,
           hg, part, ae, c_in, c_out, cx_out, cx_in, gn_keep, gn_give, gn_got, gs, gr, gx_out, gx_in,
           send_sem, recv_sem):
    ids = copy_keys(ny, nz)
    chunks, half, mid = nz // ny, ny // 2, nz // 2
    row, col = lax.axis_index("row"), lax.axis_index("col")
    y, xl = row // 2, row % 2
    z, low = col // 4, col % 4
    xh, core = low // 2, low % 2

    def at_z(o):
        return (row, lax.rem(z + (o + nz), nz) * 4 + low)

    def at_y(d):
        return (lax.rem(y + (d + ny), ny) * 2 + xl, col)

    x_lo_peer = (y * 2 + (1 - xl), col)
    x_hi_peer = (row, z * 4 + (1 - xh) * 2 + core)
    sibling = (row, z * 4 + xh * 2 + (1 - core))

    started = []

    def send(key, src, dst, device):
        copy = pltpu.make_async_remote_copy(
            src_ref=src, dst_ref=dst, send_sem=send_sem.at[ids[key]], recv_sem=recv_sem.at[ids[key]],
            device_id=device, device_id_type=pl.DeviceIdType.MESH)
        copy.start()
        started.append(copy)

    def arrived(key, dst):
        pltpu.make_async_remote_copy(
            src_ref=dst, dst_ref=dst, send_sem=send_sem.at[ids[key]], recv_sem=recv_sem.at[ids[key]],
            device_id=sibling, device_id_type=pl.DeviceIdType.MESH).wait_recv()

    barrier = pltpu.get_barrier_semaphore()
    peers = [at_y(1), at_y(-1), x_lo_peer, x_hi_peer, sibling]
    for d in range(1, mid + 1):
        peers += [at_z(d), at_z(-d)] if d < mid else [at_z(d)]
    for peer in peers:
        pl.semaphore_signal(barrier, inc=1, device_id=peer, device_id_type=pl.DeviceIdType.MESH)

    def tok(slot, rc=0, rx=0, n=1):
        return pl.ds((slot * 4 + rc * 2 + rx) * blk, n * blk)

    diagonal = lax.broadcasted_iota(jnp.int32, (blk, blk), 0) == lax.broadcasted_iota(jnp.int32, (blk, blk), 1)
    weight = jnp.sum(jnp.where(diagonal, jnp.broadcast_to(loss_weight[...], (blk, blk)), 0.0), axis=1, keepdims=True)
    hg[tok(mid), :f] = normed[...]
    hg[tok(mid), f:] = (upstream[...].astype(F32) * weight).astype(BF16)

    pl.semaphore_wait(barrier, len(peers))

    order = [o for d in range(1, mid + 1) for o in ((d, -d) if d < mid else (-d,))]
    own = hg.at[tok(mid)]
    for o in order:
        slot = (mid - o) % nz
        send(("az", slot), own, hg.at[tok(slot)], at_z(o))

    def a_x(slot):
        if slot != mid:
            arrived(("az", slot), hg.at[tok(slot)])
        send(("ax", slot), hg.at[tok(slot)], hg.at[tok(slot, rx=1)], x_hi_peer)

    def a_s(slot):
        arrived(("ax", slot), hg.at[tok(slot, rx=1)])
        send(("as", slot), hg.at[tok(slot, n=2)], hg.at[tok(slot, rc=1, n=2)], sibling)

    def a_end(slot):
        arrived(("as", slot), hg.at[tok(slot, rc=1, n=2)])

    slots_by_distance = [mid] + [(mid + o) % nz for o in order]
    base = [(mid - half + k * ny) % nz for k in range(chunks)]

    def slots_of(k):
        return [s for s in slots_by_distance if (s - base[k]) % nz < ny]

    def ranges(k):
        first = base[k]
        if first + ny <= nz:
            return [(first, ny)]
        return [(first, nz - first), (0, ny - (nz - first))]

    def products(k):
        for first, count in ranges(k):
            for s in range(first, first + count, max(1, half)):
                rows = pl.ds(s * 4 * blk, max(1, half) * 4 * blk)
                part[rows, :f] = jnp.dot(hg[rows, :f], w_in[...], preferred_element_type=F32).astype(BF16)
                part[rows, f:] = lax.dot_general(
                    hg[rows, f:], w_out[...], (((1,), (1,)), ((), ())), preferred_element_type=F32).astype(BF16)

    def owned(k, d, j):
        slot = lax.rem(base[k] + lax.rem(y + (d + ny), ny), nz)
        which = xl if j == 0 else 1 - xl
        return pl.ds(pl.multiple_of((slot * 2 + which) * (2 * blk), 2 * blk), 2 * blk)

    def stage(k, way, d, j):
        return pl.ds((((k * 2 + way) * half + d - 1) * 2 + j) * 2 * blk, 2 * blk)

    def c_step(k, d):
        for way, sign in ((0, 1), (1, -1)):
            for j in (0, 1) if d < half else (way,):
                if d == half or (d == half - 1 and j != way):
                    src = part.at[owned(k, sign * d, j)]
                else:
                    here = stage(k, way, d + 1, j)
                    arrived(("c", k, way, d + 1, j), c_in.at[here])
                    out = stage(k, way, d, j)
                    c_out[out, :] = (c_in[here, :].astype(F32) + part[owned(k, sign * d, j), :].astype(F32)).astype(BF16)
                    src = c_out.at[out]
                send(("c", k, way, d, j), src, c_in.at[stage(k, way, d, j)], at_y(sign))

    def c_total(k, j):
        total = part[owned(k, 0, j), :].astype(F32)
        for way in (0, 1):
            if half > 1 or j == way:
                here = stage(k, way, 1, j)
                arrived(("c", k, way, 1, j), c_in.at[here])
                total = total + c_in[here, :].astype(F32)
        return total

    def x_rows(k):
        return pl.ds(k * 2 * blk, 2 * blk)

    def c_cross(k):
        cx_out[x_rows(k), :] = c_total(k, 1).astype(BF16)
        send(("cx", k), cx_out.at[x_rows(k)], cx_in.at[x_rows(k)], x_lo_peer)

    def act(k):
        total = c_total(k, 0)
        arrived(("cx", k), cx_in.at[x_rows(k)])
        total = total + cx_in[x_rows(k), :].astype(F32)
        pre = total[:, :f] + b_in[...]
        cdf = 0.5 * (1.0 + lax.erf(pre * (1.0 / math.sqrt(2.0))))
        pdf = jnp.exp(-0.5 * pre * pre) * (1.0 / math.sqrt(2.0 * math.pi))
        mine = owned(k, 0, 0)
        ae[mine, :f] = (pre * cdf).astype(BF16)
        ae[mine, f:] = (total[:, f:] * (cdf + pre * pdf)).astype(BF16)
        e_send(k, 1, 0)
        send(("ex", k), ae.at[mine], ae.at[mine], x_lo_peer)

    def e_send(k, d, j):
        for way, sign in ((0, 1), (1, -1)):
            if d < half or j == way:
                rows = owned(k, -sign * (d - 1), j)
                if d > 1:
                    arrived(("e", k, way, d - 1, j), ae.at[rows])
                send(("e", k, way, d, j), ae.at[rows], ae.at[rows], at_y(sign))

    def e_cross(k):
        rows = owned(k, 0, 1)
        arrived(("ex", k), ae.at[rows])
        e_send(k, 1, 1)

    def e_step(k, d):
        e_send(k, d, 0)
        e_send(k, d, 1)

    def e_end(k):
        for way, sign in ((0, 1), (1, -1)):
            arrived(("e", k, way, half, way), ae.at[owned(k, -sign * half, way)])
            if half > 1:
                arrived(("e", k, way, half - 1, 1 - way), ae.at[owned(k, -sign * (half - 1), 1 - way)])

    def input_grad(k):
        for i, (first, count) in enumerate(ranges(k)):
            for s in range(first, first + count, max(1, half)):
                n = max(1, half)
                rows, kept = pl.ds(s * 4 * blk, n * 4 * blk), pl.ds(s * 2 * blk, n * 2 * blk)
                got = lax.dot_general(ae[rows, f:], w_in[...], (((1,), (1,)), ((), ())), preferred_element_type=F32)
                got = got.reshape(n, 2, 2 * blk, f)
                gn_keep[kept, :] = got[:, 0].reshape(n * 2 * blk, f)
                gn_give[kept, :] = got[:, 1].reshape(n * 2 * blk, f).astype(BF16)
            span = pl.ds(first * 2 * blk, count * 2 * blk)
            send(("gs", k, i), gn_give.at[span], gn_got.at[span], sibling)

    def g_send(k):
        for i, (first, count) in enumerate(ranges(k)):
            span = pl.ds(first * 2 * blk, count * 2 * blk)
            arrived(("gs", k, i), gn_got.at[span])
            gn_keep[span, :] = gn_keep[span, :] + gn_got[span, :].astype(F32)
            gs[span, :] = gn_keep[span, :].astype(BF16)
        for slot in reversed(slots_of(k)):
            if slot != mid:
                there = (2 * mid - slot) % nz
                send(("gz", there), gs.at[pl.ds(slot * 2 * blk, 2 * blk)], gr.at[pl.ds(there * 2 * blk, 2 * blk)],
                     at_z(slot - mid))

    def weight_grads(k):
        for i, (first, count) in enumerate(ranges(k)):
            rows = pl.ds(first * 4 * blk, count * 4 * blk)
            h, g = hg[rows, :f], hg[rows, f:]
            a, e = ae[rows, :f], ae[rows, f:]
            w_o = lax.dot_general(a, g, (((0,), (0,)), ((), ())), preferred_element_type=F32)
            w_i = lax.dot_general(h, e, (((0,), (0,)), ((), ())), preferred_element_type=F32)
            b = jnp.sum(e.astype(F32), axis=0, keepdims=True)
            if k == 0 and i == 0:
                o_w_out[...], o_w_in[...], o_b_in[...] = w_o, w_i, b
            else:
                o_w_out[...] += w_o
                o_w_in[...] += w_i
                o_b_in[...] += b

    def g_end():
        total = gn_keep[pl.ds(mid * 2 * blk, 2 * blk), :]
        for s in slots_by_distance[1:]:
            rows = pl.ds(s * 2 * blk, 2 * blk)
            arrived(("gz", s), gr.at[rows])
            total = total + gr[rows, :].astype(F32)
        gx_out[...] = total[blk:].astype(BF16)
        send(("gx",), gx_out, gx_in, x_hi_peer)
        arrived(("gx",), gx_in)
        o_normed[...] = (total[:blk] + gx_in[...].astype(F32)).astype(BF16)

    def gather_chunk(k):
        for s in slots_of(k):
            a_x(s)

    def spread_chunk(k):
        for s in slots_of(k):
            a_s(s)

    gather_chunk(0)
    spread_chunk(0)
    for s in slots_of(0):
        a_end(s)
    for k in range(chunks):
        products(k)
        c_step(k, half)
        if half > 1:
            c_step(k, half - 1)
        if k + 1 < chunks:
            gather_chunk(k + 1)
            spread_chunk(k + 1)
            for s in slots_of(k + 1):
                a_end(s)
    for d in range(half - 2, 0, -1):
        for k in range(chunks):
            c_step(k, d)
    for k in range(chunks):
        c_cross(k)
    for k in range(chunks):
        act(k)
    for k in range(chunks):
        e_cross(k)
    for d in range(2, half + 1):
        for k in range(chunks):
            e_step(k, d)
    for k in range(chunks):
        e_end(k)
        input_grad(k)
    for k in range(chunks):
        g_send(k)
    for k in range(chunks):
        weight_grads(k)
    g_end()
    for copy in started:
        copy.wait_send()


def on_device(ny, nz, normed, upstream, loss_weight, w_in, b_in, w_out):
    blk, f = normed.shape
    chunks, half = nz // ny, ny // 2
    n = len(copy_keys(ny, nz))
    all_rows = 4 * nz * blk
    stages = chunks * 2 * half * 2 * 2 * blk
    vmem = pl.BlockSpec(memory_space=pltpu.VMEM)
    outs = pl.pallas_call(
        functools.partial(kernel, ny, nz, blk, f),
        out_shape=(
            jax.ShapeDtypeStruct((blk, f), BF16),
            jax.ShapeDtypeStruct(w_in.shape, F32),
            jax.ShapeDtypeStruct((1, w_in.shape[1]), F32),
            jax.ShapeDtypeStruct(w_out.shape, F32),
        ),
        in_specs=[vmem] * 6,
        out_specs=(vmem,) * 4,
        scratch_shapes=[
            pltpu.VMEM((all_rows, 2 * f), BF16),
            pltpu.VMEM((all_rows, 2 * f), BF16),
            pltpu.VMEM((all_rows, 2 * f), BF16),
            pltpu.VMEM((stages, 2 * f), BF16),
            pltpu.VMEM((stages, 2 * f), BF16),
            pltpu.VMEM((chunks * 2 * blk, 2 * f), BF16),
            pltpu.VMEM((chunks * 2 * blk, 2 * f), BF16),
            pltpu.VMEM((all_rows // 2, f), F32),
            pltpu.VMEM((all_rows // 2, f), BF16),
            pltpu.VMEM((all_rows // 2, f), BF16),
            pltpu.VMEM((all_rows // 2, f), BF16),
            pltpu.VMEM((all_rows // 2, f), BF16),
            pltpu.VMEM((blk, f), BF16),
            pltpu.VMEM((blk, f), BF16),
            pltpu.SemaphoreType.DMA((n,)),
            pltpu.SemaphoreType.DMA((n,)),
        ],
        compiler_params=pltpu.CompilerParams(
            collective_id=0, has_side_effects=True, vmem_limit_bytes=48 * 2**20),
        name="mlp_backward",
    )(normed, upstream, loss_weight.reshape(1, blk), w_in, b_in.reshape(1, -1), w_out)
    return outs[0], outs[1], outs[2].reshape(-1), outs[3]


def solution(mesh):
    ny, nz = mesh.shape["row"] // 2, mesh.shape["col"] // 4
    return jax.shard_map(
        functools.partial(on_device, ny, nz),
        mesh=mesh,
        in_specs=(P("col", "row"), P("col", "row"), P("col"), P("row", "col"), P("col"), P("col", "row")),
        out_specs=(P("col", "row"), P("row", "col"), P("col"), P("col", "row")),
        check_vma=False,
    )
```

time: 522 us -> 129 us (0.25)
  the two profiles are of different devices: /device:TPU:16 before, /device:TPU:1 now
where the time goes in v1:
time: 129 us; the launch traced here: 128 us
  Pallas kernels  120 us (93%)
  local copies, waits for them, and re-layouts  6.9 us (5%)
    pallas_call x1, Pallas kernels, on_device(): pl.pallas_call(functools.partial(kernel, ny, nz, blk, f), out_shape=(jax....  120 us
    unnamed x13, local copies, waits for them, and re-layouts  6.22 us

profile of v1, /device:TPU:1, one launch (start us, length us, event | category | flops | bytes accessed | tf_op | source)
XLA Modules:
  0.0 128.2 jit_solution(13016365359105471660)
XLA Ops:
  0.6 0.7 reshape.18.b_in
  1.3 0.0 copy-start.4
  1.3 0.7 copy-done.4
  2.0 0.0 copy-start
  2.0 1.0 copy-done
  2.9 0.0 copy-start.1
  2.9 1.0 copy-done.1
  3.9 0.0 copy-start.2
  3.9 0.7 copy-done.2
  4.6 0.0 copy-start.3
  4.6 0.7 copy-done.3
  5.3 120.0 %mlp_backward.1 = (bf16[16,384]{1,0:T(8,128)(2,1)S(1)}, f32[384,384]{1,0:T(8,128)S(1)}, f32[1,384]{1,0:T(1,128)S(1)}, f32[384,384]{1,0:T(8,128)S(1)}) custom-call(bf16[16,384]{1,0:T(8,128)(2,1)S(1)} %copy-done.2, bf16[16,384]{1,0:T(8,128)(2,1)S(1)} %copy-done.3, f32[1,16]{1,0:T(1,128)S(1)} %bitcast.1, bf16[384,384]{1,0:T(8,128)(2,1)S(1)} %copy-done, ...), custom_call_target="tpu_custom_call" | custom-call | tf_op jit(solution)/shard_map/mlp_backward/pallas_call | solution.py:297
  125.4 0.6 reduce
  126.0 0.6 copy.13
  126.6 0.8 copy.14
  127.4 0.8 copy.15
Async XLA Ops:
  1.3 0.7 copy-start.4
  2.0 1.0 copy-start
  2.9 1.0 copy-start.1
  3.9 0.7 copy-start.2
  4.6 0.7 copy-start.3

commit v2 on v0

v2 whole, which is shorter than its diff:
```python
import functools
import math

import jax
import jax.numpy as jnp
from jax import lax
from jax.experimental import pallas as pl
from jax.experimental.pallas import tpu as pltpu
from jax.sharding import PartitionSpec as P

BF16 = jnp.bfloat16
F32 = jnp.float32
MESH = pl.DeviceIdType.MESH


def copy_keys(ny, nz):
    half, reach = ny // 2, nz // 4
    ways = (0, 1)
    keys = [("wi",), ("wo",), ("al",)]
    keys += [("az", s, rx) for rx in ways for s in range(1, nz) if s != nz // 2]
    keys += [("az", 0, rx, way) for rx in ways for way in ways]
    keys += [("al", nz // 2 + s * d) for d in range(1, reach + 1) for s in (1, -1)]
    keys += [("ax", nz // 2 + d) for d in range(-reach, reach + 1)] + [("as", s) for s in range(nz)]
    keys += [(kind, way, i) for kind in ("c1", "c2", "e1", "e2") for way in ways for i in range(1, half // 2 + 1)]
    keys += [("gs", i) for i in ways]
    keys += [(kind, way, i) for kind in ("g1", "g2") for way in ways for i in range(1, reach + 1)]
    keys += [("gx",), ("gl",), ("gd",), ("vi",), ("vo",), ("vb",)]
    return {key: i for i, key in enumerate(keys)}


def kernel(ny, nz, blk, f, normed_hbm, upstream_hbm, loss_weight_hbm, w_in_hbm, b_in_hbm, w_out_hbm,
           o_normed, o_w_in, o_b_in, o_w_out,
           normed, upstream, loss_weight, b_in, w_in, w_out, w_in2, w_out2,
           hg, al_out, part, ae, c1_in, c2_out, c2_in, gn, gn_give, gn_got, gs, g1_in, g2_out, g2_in, g_out, gx_in, gl_in, gd_in,
           vi_out, vi_in, vo_out, vo_in, vb_out, vb_in, load_sem, send_sem, recv_sem):
    ids = copy_keys(ny, nz)
    half, mid, reach = ny // 2, nz // 2, nz // 4
    hop = half // 2
    row, col = lax.axis_index("row"), lax.axis_index("col")
    y, xl = row // 2, row % 2
    z, low = col // 4, col % 4
    xh, core = low // 2, low % 2
    busy = core == xl
    idle = core != xl
    signs = ((0, 1), (1, -1))

    def at_z(o):
        return (row, lax.rem(z + (o + nz), nz) * 4 + low)

    def at_y(d):
        return (lax.rem(y + (d + ny), ny) * 2 + xl, col)

    x_lo_peer = (y * 2 + (1 - xl), col)
    x_hi_peer = (row, z * 4 + (1 - xh) * 2 + core)
    x_both_peer = (y * 2 + (1 - xl), z * 4 + (1 - xh) * 2 + core)
    sibling = (row, z * 4 + xh * 2 + (1 - core))

    sent = {"all": [], "busy": [], "idle": []}

    def send(key, src, dst, device, who="all"):
        pltpu.make_async_remote_copy(
            src_ref=src, dst_ref=dst, send_sem=send_sem.at[ids[key]], recv_sem=recv_sem.at[ids[key]],
            device_id=device, device_id_type=MESH).start()
        sent[who].append((key, src))

    def handle(key, ref):
        return pltpu.make_async_remote_copy(
            src_ref=ref, dst_ref=ref, send_sem=send_sem.at[ids[key]], recv_sem=recv_sem.at[ids[key]],
            device_id=sibling, device_id_type=MESH)

    def arrived(key, dst):
        handle(key, dst).wait_recv()

    barrier = pltpu.get_barrier_semaphore()
    toward = [s * d for d in range(reach, 0, -1) for s in (1, -1)]
    near = [at_y(sign * d) for d in range(1, hop + 1) for sign in (1, -1)]
    near += [x_lo_peer, x_hi_peer, x_both_peer, sibling]
    along_z = [at_z(o) for o in toward]
    slanted = [(y * 2 + (1 - xl), at_z(o)[1]) for o in toward]
    for peer in slanted + near:
        pl.semaphore_signal(barrier, inc=1, device_id=peer, device_id_type=MESH)

    @pl.when(busy)
    def _():
        for peer in along_z:
            pl.semaphore_signal(barrier, inc=1, device_id=peer, device_id_type=MESH)

    pairs = ((normed_hbm, normed), (upstream_hbm, upstream), (loss_weight_hbm, loss_weight), (b_in_hbm, b_in),
             (w_in_hbm, w_in), (w_out_hbm, w_out))
    loads = [pltpu.make_async_copy(src, dst, load_sem.at[i]) for i, (src, dst) in enumerate(pairs)]
    for load in loads:
        load.start()
    for load in loads[:4]:
        load.wait()

    def tok(slot, rx=0, n=1):
        return pl.ds((slot * 2 + rx) * blk, n * blk)

    diagonal = lax.broadcasted_iota(jnp.int32, (blk, blk), 0) == lax.broadcasted_iota(jnp.int32, (blk, blk), 1)
    weight = jnp.sum(jnp.where(diagonal, jnp.broadcast_to(loss_weight[...], (blk, blk)), 0.0), axis=1, keepdims=True)
    weighted = (upstream[...].astype(F32) * weight).astype(BF16)

    slab0, slab1 = pl.ds(0, 2 * f), pl.ds(2 * f, 2 * f)
    first_slots = [mid + s * d for d in range(1, reach) for s in (1, -1)]
    far_slots = [mid + s * d for d in range(reach + 1, mid) for s in (1, -1)] + [0]
    edge_slots = [mid - reach, mid + reach]

    @pl.when(idle)
    def _():
        al_out[:, :f] = normed[...]
        al_out[:, f:] = weighted
        pl.semaphore_wait(barrier, len(near) + len(slanted))
        for o, peer in zip(toward, slanted):
            send(("al", mid - o), al_out, hg.at[tok(mid - o), slab1], peer, "idle")
        send(("al",), al_out, hg.at[tok(mid), slab1], x_lo_peer, "idle")
        send(("wi",), w_in_hbm, w_in2, x_lo_peer, "idle")
        send(("wo",), w_out_hbm, w_out2, x_lo_peer, "idle")

    @pl.when(busy)
    def _():
        hg[tok(mid), slab0] = jnp.concatenate([normed[...], weighted], axis=1)
        pl.semaphore_wait(barrier, len(near) + len(slanted) + len(along_z))
        for o, peer in zip(toward, along_z):
            send(("az", mid - o, 0), hg.at[tok(mid), slab0], hg.at[tok(mid - o), slab0], peer, "busy")

    def relay(way, sign, rx):
        slot = mid - sign * reach
        for d in range(reach, 0, -1):
            there = (slot - sign * d) % nz
            src, dst = tok(slot, rx), tok(there, rx)
            if d < reach:
                send(("az", there, rx), hg.at[src], hg.at[dst], at_z(sign * d), "busy")
            else:
                lanes = pl.ds(2 * f * way, 2 * f)
                send(("az", 0, rx, way), hg.at[src, lanes], hg.at[dst, lanes], at_z(sign * d), "busy")

    @pl.when(busy)
    def _():
        def meet(slot):
            if slot != mid:
                arrived(("az", slot, 0), hg.at[tok(slot), slab0])
            arrived(("al",) if slot == mid else ("al", slot), hg.at[tok(slot), slab1])
            send(("ax", slot), hg.at[tok(slot)], hg.at[tok(slot, rx=1)], x_hi_peer, "busy")

        def down(slot):
            send(("as", slot), hg.at[tok(slot, n=2)], hg.at[tok(slot, n=2)], sibling, "busy")

        for way, sign in signs:
            meet(mid - sign * reach)
            relay(way, sign, 0)
        for s in [mid] + first_slots:
            meet(s)
        send(("wi",), w_in_hbm, w_in2, x_lo_peer, "busy")
        send(("wo",), w_out_hbm, w_out2, x_lo_peer, "busy")
        for way, sign in signs:
            slot = mid - sign * reach
            arrived(("ax", slot), hg.at[tok(slot, rx=1)])
            relay(way, sign, 1)
            down(slot)
        for s in [mid] + first_slots:
            arrived(("ax", s), hg.at[tok(s, rx=1)])
            down(s)
        for s in far_slots:
            for rx in (0, 1):
                if s == 0:
                    for way in (0, 1):
                        arrived(("az", 0, rx, way), hg.at[tok(0, rx), pl.ds(2 * f * way, 2 * f)])
                else:
                    arrived(("az", s, rx), hg.at[tok(s, rx)])
            down(s)

    @pl.when(idle)
    def _():
        for s in range(nz):
            arrived(("as", s), hg.at[tok(s, n=2)])

    def products():
        part[:, :f] = (jnp.dot(hg[:, :f], w_in[...], preferred_element_type=F32)
                       + jnp.dot(hg[:, 2 * f:3 * f], w_in2[...], preferred_element_type=F32)).astype(BF16)
        turned = (((1,), (1,)), ((), ()))
        part[:, f:] = (
            lax.dot_general(hg[:, f:2 * f], w_out[...], turned, preferred_element_type=F32)
            + lax.dot_general(hg[:, 3 * f:], w_out2[...], turned, preferred_element_type=F32)).astype(BF16)

    share = 2 * nz * blk // ny

    def owned(d, j=None):
        start = lax.rem(y + (d + ny), ny) * share
        if j is None:
            return pl.ds(pl.multiple_of(start, share), share)
        return pl.ds(pl.multiple_of(start + j * (share // 2), share // 2), share // 2)

    def stage(way, i, j=None):
        start = (way * hop + i - 1) * share
        return pl.ds(start, share) if j is None else pl.ds(start + j * (share // 2), share // 2)

    def c_first():
        for i in range(hop, 0, -1):
            for way, sign in signs:
                j = way if i == hop else None
                send(("c1", way, i), part.at[owned(sign * (hop + i), j)], c1_in.at[stage(way, i, j)], at_y(sign * i))
        for i in range(hop - 1, 0, -1):
            for way, sign in signs:
                send(("c2", way, i), part.at[owned(sign * i)], c2_in.at[stage(way, i)], at_y(sign * i))

    def c_relay():
        for way, sign in signs:
            out = pl.ds(way * share, share)
            last = stage(way, hop, way)
            total = part[owned(sign * hop), :].astype(F32)
            for i in range(1, hop):
                arrived(("c1", way, i), c1_in.at[stage(way, i)])
                total = total + c1_in[stage(way, i), :].astype(F32)
            arrived(("c1", way, hop), c1_in.at[last])
            c2_out[out, :] = total.astype(BF16)
            lo = way * (share // 2)
            c2_out[pl.ds(way * share + lo, share // 2), :] = (
                total[lo:lo + share // 2] + c1_in[last, :].astype(F32)).astype(BF16)
            send(("c2", way, hop), c2_out.at[out], c2_in.at[stage(way, hop)], at_y(sign * hop))

    def act():
        mine = owned(0)
        total = part[mine, :].astype(F32)
        for i in range(1, hop + 1):
            for way in (0, 1):
                arrived(("c2", way, i), c2_in.at[stage(way, i)])
                total = total + c2_in[stage(way, i), :].astype(F32)
        pre = total[:, :f] + b_in[...].reshape(1, f)
        cdf = 0.5 * (1.0 + lax.erf(pre * (1.0 / math.sqrt(2.0))))
        pdf = jnp.exp(-0.5 * pre * pre) * (1.0 / math.sqrt(2.0 * math.pi))
        ae[mine, :f] = (pre * cdf).astype(BF16)
        ae[mine, f:] = (total[:, f:] * (cdf + pre * pdf)).astype(BF16)
        for i in range(hop, 0, -1):
            for way, sign in signs:
                send(("e1", way, i), ae.at[mine], ae.at[mine], at_y(sign * i))

    def e_relay():
        for way, sign in signs:
            arrived(("e1", way, hop), ae.at[owned(-sign * hop)])
            for d in range(hop, 0, -1):
                rows = owned(-sign * hop, way if d == hop else None)
                send(("e2", way, d), ae.at[rows], ae.at[rows], at_y(sign * d))

    def e_end():
        for way, sign in signs:
            for i in range(1, hop):
                arrived(("e1", way, i), ae.at[owned(-sign * i)])
            for d in range(1, hop + 1):
                arrived(("e2", way, d), ae.at[owned(-sign * (hop + d), way if d == hop else None)])

    pieces = [(i, pl.ds(i * nz * blk, nz * blk)) for i in (0, 1)]

    def input_grad():
        turned = (((1,), (1,)), ((), ()))
        for i, rows in pieces:
            own = lax.dot_general(ae[rows, f:], w_in[...], turned, preferred_element_type=F32)
            other = lax.dot_general(ae[rows, f:], w_in2[...], turned, preferred_element_type=F32)

            @pl.when(busy)
            def _():
                gn[rows, :f] = own
                gn[rows, f:] = other

            @pl.when(idle)
            def _():
                gn_give[rows, :f] = own.astype(BF16)
                gn_give[rows, f:] = other.astype(BF16)
                send(("gs", i), gn_give.at[rows], gn_got.at[rows], sibling, "idle")

    def g_first():
        for i, rows in pieces:
            arrived(("gs", i), gn_got.at[rows])
            gn[rows, :] = gn[rows, :] + gn_got[rows, :].astype(F32)
            gs[rows, :] = gn[rows, :].astype(BF16)

    def g_rows(way, i, j=None):
        start = (way * reach + i - 1) * 2 * blk
        return pl.ds(start, 2 * blk) if j is None else pl.ds(start + j * blk, blk)

    def g_send():
        for i in range(reach, 0, -1):
            for way, sign in signs:
                slot = (mid + sign * (reach + i)) % nz
                src, dst = (tok(slot, n=2), g_rows(way, i)) if i < reach else (tok(slot, rx=way), g_rows(way, i, way))
                send(("g1", way, i), gs.at[src], g1_in.at[dst], at_z(sign * i), "busy")
        for i in range(reach - 1, 0, -1):
            for way, sign in signs:
                send(("g2", way, i), gs.at[tok(mid + sign * i, n=2)], g2_in.at[g_rows(way, i)], at_z(sign * i), "busy")

    def g_relay():
        for way, sign in signs:
            total = gn[tok(mid + sign * reach, n=2), :]
            for i in range(1, reach):
                arrived(("g1", way, i), g1_in.at[g_rows(way, i)])
                total = total + g1_in[g_rows(way, i), :].astype(F32)
            last = g_rows(way, reach, way)
            arrived(("g1", way, reach), g1_in.at[last])
            there, out = g_rows(way, reach), pl.ds(way * 2 * blk, 2 * blk)
            g2_out[out, :] = total.astype(BF16)
            half_rows = pl.ds((way * 2 + way) * blk, blk)
            g2_out[half_rows, :] = (total[way * blk:(way + 1) * blk] + g1_in[last, :].astype(F32)).astype(BF16)
            send(("g2", way, reach), g2_out.at[out], g2_in.at[there], at_z(sign * reach), "busy")

    def g_end():
        total = gn[tok(mid, n=2), :]
        for i in range(1, reach + 1):
            for way in (0, 1):
                arrived(("g2", way, i), g2_in.at[g_rows(way, i)])
                total = total + g2_in[g_rows(way, i), :].astype(F32)
        g_out[...] = total.astype(BF16)
        send(("gx",), g_out.at[pl.ds(blk, blk), pl.ds(0, f)], gx_in, x_hi_peer, "busy")
        send(("gl",), g_out.at[pl.ds(0, blk), pl.ds(f, f)], gl_in, x_lo_peer, "busy")
        send(("gd",), g_out.at[pl.ds(blk, blk), pl.ds(f, f)], gd_in, x_both_peer, "busy")
        arrived(("gx",), gx_in)
        o_normed[...] = (total[:blk, :f] + gx_in[...].astype(F32)).astype(BF16)

    down_rows = (((0,), (0,)), ((), ()))

    def other_weight_grads():
        a, e = ae[:, :f], ae[:, f:]
        vo_out[...] = lax.dot_general(a, hg[:, 3 * f:], down_rows, preferred_element_type=F32).astype(BF16)
        send(("vo",), vo_out, vo_in, x_lo_peer)
        vi_out[...] = lax.dot_general(hg[:, 2 * f:3 * f], e, down_rows, preferred_element_type=F32).astype(BF16)
        send(("vi",), vi_out, vi_in, x_lo_peer)
        vb_out[...] = jnp.broadcast_to(jnp.sum(e.astype(F32), axis=0, keepdims=True), (8, f))
        send(("vb",), vb_out, vb_in, x_lo_peer)

    def weight_grads():
        a, e = ae[:, :f], ae[:, f:]
        o_w_out[...] = lax.dot_general(a, hg[:, f:2 * f], down_rows, preferred_element_type=F32)
        o_w_in[...] = lax.dot_general(hg[:, :f], e, down_rows, preferred_element_type=F32)

    def weight_grads_end():
        arrived(("vo",), vo_in)
        o_w_out[...] += vo_in[...].astype(F32)
        arrived(("vi",), vi_in)
        o_w_in[...] += vi_in[...].astype(F32)
        arrived(("vb",), vb_in)
        o_b_in[...] = (vb_out[:1, :] + vb_in[:1, :]).reshape(f)

    for load in loads[4:]:
        load.wait()
    arrived(("wi",), w_in2)
    arrived(("wo",), w_out2)
    products()
    c_first()
    c_relay()
    act()
    e_relay()
    e_end()
    input_grad()

    @pl.when(busy)
    def _():
        g_first()
        g_send()

    other_weight_grads()

    @pl.when(busy)
    def _():
        g_relay()

    weight_grads()
    weight_grads_end()

    @pl.when(busy)
    def _():
        g_end()

    @pl.when(idle)
    def _():
        arrived(("gl",), gl_in)
        arrived(("gd",), gd_in)
        o_normed[...] = (gl_in[...].astype(F32) + gd_in[...].astype(F32)).astype(BF16)
        for key, src in sent["idle"]:
            handle(key, src).wait_send()

    @pl.when(busy)
    def _():
        for key, src in sent["busy"]:
            handle(key, src).wait_send()

    for key, src in sent["all"]:
        handle(key, src).wait_send()


def on_device(ny, nz, normed, upstream, loss_weight, w_in, b_in, w_out):
    blk, f = normed.shape
    half, reach = ny // 2, nz // 4
    n = len(copy_keys(ny, nz))
    rows = 2 * nz * blk
    share = rows // ny
    vmem, hbm = pl.BlockSpec(memory_space=pltpu.VMEM), pl.BlockSpec(memory_space=pl.ANY)
    outs = pl.pallas_call(
        functools.partial(kernel, ny, nz, blk, f),
        out_shape=(
            jax.ShapeDtypeStruct((blk, f), BF16),
            jax.ShapeDtypeStruct(w_in.shape, F32),
            jax.ShapeDtypeStruct((f,), F32),
            jax.ShapeDtypeStruct(w_out.shape, F32),
        ),
        in_specs=[hbm] * 6,
        out_specs=(vmem,) * 4,
        scratch_shapes=[
            pltpu.VMEM((blk, f), BF16),
            pltpu.VMEM((blk, f), BF16),
            pltpu.VMEM((1, blk), F32),
            pltpu.VMEM((f,), F32),
            pltpu.VMEM((f, f), BF16),
            pltpu.VMEM((f, f), BF16),
            pltpu.VMEM((f, f), BF16),
            pltpu.VMEM((f, f), BF16),
            pltpu.VMEM((rows, 4 * f), BF16),
            pltpu.VMEM((blk, 2 * f), BF16),
            pltpu.VMEM((rows, 2 * f), BF16),
            pltpu.VMEM((rows, 2 * f), BF16),
            pltpu.VMEM((half * share, 2 * f), BF16),
            pltpu.VMEM((2 * share, 2 * f), BF16),
            pltpu.VMEM((half * share, 2 * f), BF16),
            pltpu.VMEM((rows, 2 * f), F32),
            pltpu.VMEM((rows, 2 * f), BF16),
            pltpu.VMEM((rows, 2 * f), BF16),
            pltpu.VMEM((rows, 2 * f), BF16),
            pltpu.VMEM((2 * reach * 2 * blk, 2 * f), BF16),
            pltpu.VMEM((2 * 2 * blk, 2 * f), BF16),
            pltpu.VMEM((2 * reach * 2 * blk, 2 * f), BF16),
            pltpu.VMEM((2 * blk, 2 * f), BF16),
            pltpu.VMEM((blk, f), BF16),
            pltpu.VMEM((blk, f), BF16),
            pltpu.VMEM((blk, f), BF16),
            pltpu.VMEM((f, f), BF16),
            pltpu.VMEM((f, f), BF16),
            pltpu.VMEM((f, f), BF16),
            pltpu.VMEM((f, f), BF16),
            pltpu.VMEM((8, f), F32),
            pltpu.VMEM((8, f), F32),
            pltpu.SemaphoreType.DMA((6,)),
            pltpu.SemaphoreType.DMA((n,)),
            pltpu.SemaphoreType.DMA((n,)),
        ],
        compiler_params=pltpu.CompilerParams(
            collective_id=0, has_side_effects=True, vmem_limit_bytes=60 * 2**20),
        name="mlp_backward",
    )(normed, upstream, loss_weight.reshape(1, blk), w_in, b_in, w_out)
    return outs[0], outs[1], outs[2], outs[3]


def solution(mesh):
    ny, nz = mesh.shape["row"] // 2, mesh.shape["col"] // 4
    return jax.shard_map(
        functools.partial(on_device, ny, nz),
        mesh=mesh,
        in_specs=(P("col", "row"), P("col", "row"), P("col"), P("row", "col"), P("col"), P("col", "row")),
        out_specs=(P("col", "row"), P("row", "col"), P("col"), P("col", "row")),
        check_vma=False,
    )
```

time: 522 us -> 95.7 us (0.18)
  the two profiles are of different devices: /device:TPU:16 before, /device:TPU:8 now
where the time goes in v2:
time: 95.7 us; the launch traced here: 95.4 us
  Pallas kernels  90.1 us (94%)
  local copies, waits for them, and re-layouts  4.69 us (5%)
    pallas_call x1, Pallas kernels, on_device(): pl.pallas_call(functools.partial(kernel, ny, nz, blk, f), out_shape=(jax....  90.1 us
    unnamed x8, local copies, waits for them, and re-layouts  4.69 us

profile of v2, /device:TPU:8, one launch (start us, length us, event | category | flops | bytes accessed | tf_op | source)
XLA Modules:
  0.0 95.4 jit_solution(11956370718108542332)
XLA Ops:
  0.6 90.1 %mlp_backward.1 = (bf16[16,384]{1,0:T(8,128)(2,1)}, f32[384,384]{1,0:T(8,128)}, f32[384]{0:T(512)}, f32[384,384]{1,0:T(8,128)}) custom-call(bf16[16,384]{1,0:T(8,128)(2,1)} %normed_hbm.1, bf16[16,384]{1,0:T(8,128)(2,1)} %upstream_hbm.1, f32[1,16]{1,0:T(1,128)} %bitcast.1, bf16[384,384]{1,0:T(8,128)(2,1)} %w_in_hbm.1, f32[384]{0:T(512)} %b_in_hbm.1, ...), custom_call_target="tpu_custom_call" | custom-call | tf_op jit(solution)/shard_map/mlp_backward/pallas_call | solution.py:395
  90.8 1.3 %copy.14 = bf16[16,384]{1,0:T(8,128)(2,1)} copy(bf16[16,384]{1,0:T(8,128)(2,1)} %get-tuple-element.8) | data formatting | bytes 24576
  92.1 0.0 copy-start.1
  92.1 0.0 copy-start
  92.1 2.0 %copy.15 = f32[384,384]{1,0:T(8,128)} copy(f32[384,384]{1,0:T(8,128)} %get-tuple-element.9) | data formatting | bytes 1179648
  94.0 0.0 copy-done.1
  94.0 0.6 copy.16
  94.6 0.0 copy-done
  94.6 0.8 copy.17
Async XLA Ops:
  92.1 2.0 %copy-start.1 = (f32[384]{0:T(512)S(1)}, f32[384]{0:T(512)}, u32[]{:S(2)}) copy-start(f32[384]{0:T(512)} %get-tuple-element.10) | copy-start | bytes 4612
  92.1 2.6 %copy-start = (f32[384,384]{1,0:T(8,128)S(1)}, f32[384,384]{1,0:T(8,128)}, u32[]{:S(2)}) copy-start(f32[384,384]{1,0:T(8,128)} %get-tuple-element.11) | copy-start | bytes 1769476

commit v3 on v2

--- a/solution.py
+++ b/solution.py
@@ -20,18 +20,18 @@
     keys += [("az", s, rx) for rx in ways for s in range(1, nz) if s != nz // 2]
     keys += [("az", 0, rx, way) for rx in ways for way in ways]
     keys += [("al", nz // 2 + s * d) for d in range(1, reach + 1) for s in (1, -1)]
-    keys += [("ax", nz // 2 + d) for d in range(-reach, reach + 1)] + [("as", s) for s in range(nz)]
+    keys += [("ax", nz // 2 + d) for d in range(-reach, reach + 1)] + [("as", i) for i in range(3)]
     keys += [(kind, way, i) for kind in ("c1", "c2", "e1", "e2") for way in ways for i in range(1, half // 2 + 1)]
-    keys += [("gs", i) for i in ways]
+    keys += [("gs", d % ny) for d in range(ny)]
     keys += [(kind, way, i) for kind in ("g1", "g2") for way in ways for i in range(1, reach + 1)]
-    keys += [("gx",), ("gl",), ("gd",), ("vi",), ("vo",), ("vb",)]
+    keys += [("gx",), ("gl",), ("vi",), ("vo",), ("vb",)]
     return {key: i for i, key in enumerate(keys)}
 
 
 def kernel(ny, nz, blk, f, normed_hbm, upstream_hbm, loss_weight_hbm, w_in_hbm, b_in_hbm, w_out_hbm,
            o_normed, o_w_in, o_b_in, o_w_out,
-           normed, upstream, loss_weight, b_in, w_in, w_out, w_in2, w_out2,
-           hg, al_out, part, ae, c1_in, c2_out, c2_in, gn, gn_give, gn_got, gs, g1_in, g2_out, g2_in, g_out, gx_in, gl_in, gd_in,
+           normed, upstream, loss_weight, b_in, w_in, w_out, w_in2, w_out2, turned_in,
+           hg, al_out, part, ae, c1_in, c2_out, c2_in, gn, gn_give, gn_got, gs, g1_in, g2_out, g2_in, g_out, gx_in, gl_in,
            vi_out, vi_in, vo_out, vo_in, vb_out, vb_in, load_sem, send_sem, recv_sem):
     ids = copy_keys(ny, nz)
     half, mid, reach = ny // 2, nz // 2, nz // 4
@@ -52,7 +52,8 @@
 
     x_lo_peer = (y * 2 + (1 - xl), col)
     x_hi_peer = (row, z * 4 + (1 - xh) * 2 + core)
-    x_both_peer = (y * 2 + (1 - xl), z * 4 + (1 - xh) * 2 + core)
+    cross_lo = (y * 2 + (1 - xl), z * 4 + xh * 2 + (1 - core))
+    cross_both = (y * 2 + (1 - xl), z * 4 + (1 - xh) * 2 + (1 - core))
     sibling = (row, z * 4 + xh * 2 + (1 - core))
 
     sent = {"all": [], "busy": [], "idle": []}
@@ -74,15 +75,16 @@
     barrier = pltpu.get_barrier_semaphore()
     toward = [s * d for d in range(reach, 0, -1) for s in (1, -1)]
     near = [at_y(sign * d) for d in range(1, hop + 1) for sign in (1, -1)]
-    near += [x_lo_peer, x_hi_peer, x_both_peer, sibling]
+    near += [x_lo_peer, x_hi_peer, sibling] + [at_z(o) for o in toward]
     along_z = [at_z(o) for o in toward]
     slanted = [(y * 2 + (1 - xl), at_z(o)[1]) for o in toward]
+    crossed = [cross_lo, cross_both]
     for peer in slanted + near:
         pl.semaphore_signal(barrier, inc=1, device_id=peer, device_id_type=MESH)
 
-    @pl.when(busy)
-    def _():
-        for peer in along_z:
+    @pl.when(idle)
+    def _():
+        for peer in crossed:
             pl.semaphore_signal(barrier, inc=1, device_id=peer, device_id_type=MESH)
 
     pairs = ((normed_hbm, normed), (upstream_hbm, upstream), (loss_weight_hbm, loss_weight), (b_in_hbm, b_in),
@@ -102,14 +104,13 @@
 
     slab0, slab1 = pl.ds(0, 2 * f), pl.ds(2 * f, 2 * f)
     first_slots = [mid + s * d for d in range(1, reach) for s in (1, -1)]
-    far_slots = [mid + s * d for d in range(reach + 1, mid) for s in (1, -1)] + [0]
-    edge_slots = [mid - reach, mid + reach]
+    spans = [(mid - reach, 2 * reach + 1), (mid + reach + 1, mid - reach - 1), (0, mid - reach)]
 
     @pl.when(idle)
     def _():
         al_out[:, :f] = normed[...]
         al_out[:, f:] = weighted
-        pl.semaphore_wait(barrier, len(near) + len(slanted))
+        pl.semaphore_wait(barrier, len(near) + len(slanted) + len(crossed))
         for o, peer in zip(toward, slanted):
             send(("al", mid - o), al_out, hg.at[tok(mid - o), slab1], peer, "idle")
         send(("al",), al_out, hg.at[tok(mid), slab1], x_lo_peer, "idle")
@@ -119,7 +120,7 @@
     @pl.when(busy)
     def _():
         hg[tok(mid), slab0] = jnp.concatenate([normed[...], weighted], axis=1)
-        pl.semaphore_wait(barrier, len(near) + len(slanted) + len(along_z))
+        pl.semaphore_wait(barrier, len(near) + len(slanted))
         for o, peer in zip(toward, along_z):
             send(("az", mid - o, 0), hg.at[tok(mid), slab0], hg.at[tok(mid - o), slab0], peer, "busy")
 
@@ -142,8 +143,9 @@
             arrived(("al",) if slot == mid else ("al", slot), hg.at[tok(slot), slab1])
             send(("ax", slot), hg.at[tok(slot)], hg.at[tok(slot, rx=1)], x_hi_peer, "busy")
 
-        def down(slot):
-            send(("as", slot), hg.at[tok(slot, n=2)], hg.at[tok(slot, n=2)], sibling, "busy")
+        def down(i):
+            rows = tok(spans[i][0], n=2 * spans[i][1])
+            send(("as", i), hg.at[rows], hg.at[rows], sibling, "busy")
 
         for way, sign in signs:
             meet(mid - sign * reach)
@@ -156,23 +158,24 @@
             slot = mid - sign * reach
             arrived(("ax", slot), hg.at[tok(slot, rx=1)])
             relay(way, sign, 1)
-            down(slot)
         for s in [mid] + first_slots:
             arrived(("ax", s), hg.at[tok(s, rx=1)])
-            down(s)
-        for s in far_slots:
-            for rx in (0, 1):
-                if s == 0:
-                    for way in (0, 1):
-                        arrived(("az", 0, rx, way), hg.at[tok(0, rx), pl.ds(2 * f * way, 2 * f)])
-                else:
-                    arrived(("az", s, rx), hg.at[tok(s, rx)])
-            down(s)
+        down(0)
+        for i in (1, 2):
+            for s in range(spans[i][0], spans[i][0] + spans[i][1]):
+                for rx in (0, 1):
+                    if s == 0:
+                        for way in (0, 1):
+                            arrived(("az", 0, rx, way), hg.at[tok(0, rx), pl.ds(2 * f * way, 2 * f)])
+                    else:
+                        arrived(("az", s, rx), hg.at[tok(s, rx)])
+            down(i)
 
     @pl.when(idle)
     def _():
-        for s in range(nz):
-            arrived(("as", s), hg.at[tok(s, n=2)])
+        for i in range(3):
+            rows = tok(spans[i][0], n=2 * spans[i][1])
+            arrived(("as", i), hg.at[rows])
 
     def products():
         part[:, :f] = (jnp.dot(hg[:, :f], w_in[...], preferred_element_type=F32)
@@ -241,37 +244,55 @@
                 rows = owned(-sign * hop, way if d == hop else None)
                 send(("e2", way, d), ae.at[rows], ae.at[rows], at_y(sign * d))
 
-    def e_end():
-        for way, sign in signs:
-            for i in range(1, hop):
+    def input_grad(d):
+        rows = owned(d)
+        both = jnp.dot(ae[rows, f:], turned_in[...], preferred_element_type=F32)
+        own, other = both[:, :f], both[:, f:]
+
+        @pl.when(busy)
+        def _():
+            gn[rows, :] = own
+            gn_give[rows, :] = other.astype(BF16)
+
+        @pl.when(idle)
+        def _():
+            gn[rows, :] = other
+            gn_give[rows, :] = own.astype(BF16)
+
+        send(("gs", d % ny), gn_give.at[rows], gn_got.at[rows], sibling)
+
+    def g_first(d):
+        rows = owned(d)
+        arrived(("gs", d % ny), gn_got.at[rows])
+        gn[rows, :] = gn[rows, :] + gn_got[rows, :].astype(F32)
+        gs[rows, :] = gn[rows, :].astype(BF16)
+
+    def gather_and_grad():
+        input_grad(0)
+        e_relay()
+        for way, sign in signs:
+            input_grad(-sign * hop)
+        g_first(0)
+        for i in range(1, hop):
+            for way, sign in signs:
                 arrived(("e1", way, i), ae.at[owned(-sign * i)])
-            for d in range(1, hop + 1):
-                arrived(("e2", way, d), ae.at[owned(-sign * (hop + d), way if d == hop else None)])
-
-    pieces = [(i, pl.ds(i * nz * blk, nz * blk)) for i in (0, 1)]
-
-    def input_grad():
-        turned = (((1,), (1,)), ((), ()))
-        for i, rows in pieces:
-            own = lax.dot_general(ae[rows, f:], w_in[...], turned, preferred_element_type=F32)
-            other = lax.dot_general(ae[rows, f:], w_in2[...], turned, preferred_element_type=F32)
-
-            @pl.when(busy)
-            def _():
-                gn[rows, :f] = own
-                gn[rows, f:] = other
-
-            @pl.when(idle)
-            def _():
-                gn_give[rows, :f] = own.astype(BF16)
-                gn_give[rows, f:] = other.astype(BF16)
-                send(("gs", i), gn_give.at[rows], gn_got.at[rows], sibling, "idle")
-
-    def g_first():
-        for i, rows in pieces:
-            arrived(("gs", i), gn_got.at[rows])
-            gn[rows, :] = gn[rows, :] + gn_got[rows, :].astype(F32)
-            gs[rows, :] = gn[rows, :].astype(BF16)
+                input_grad(-sign * i)
+        for way, sign in signs:
+            g_first(-sign * hop)
+        for d in range(1, hop):
+            for way, sign in signs:
+                arrived(("e2", way, d), ae.at[owned(-sign * (hop + d))])
+                input_grad(-sign * (hop + d))
+        for i in range(1, hop):
+            for way, sign in signs:
+                g_first(-sign * i)
+        for way, sign in signs:
+            arrived(("e2", way, hop), ae.at[owned(half, way)])
+        input_grad(half)
+        for d in range(1, hop):
+            for way, sign in signs:
+                g_first(-sign * (hop + d))
+        g_first(half)
 
     def g_rows(way, i, j=None):
         start = (way * reach + i - 1) * 2 * blk
@@ -282,10 +303,10 @@
             for way, sign in signs:
                 slot = (mid + sign * (reach + i)) % nz
                 src, dst = (tok(slot, n=2), g_rows(way, i)) if i < reach else (tok(slot, rx=way), g_rows(way, i, way))
-                send(("g1", way, i), gs.at[src], g1_in.at[dst], at_z(sign * i), "busy")
+                send(("g1", way, i), gs.at[src], g1_in.at[dst], at_z(sign * i))
         for i in range(reach - 1, 0, -1):
             for way, sign in signs:
-                send(("g2", way, i), gs.at[tok(mid + sign * i, n=2)], g2_in.at[g_rows(way, i)], at_z(sign * i), "busy")
+                send(("g2", way, i), gs.at[tok(mid + sign * i, n=2)], g2_in.at[g_rows(way, i)], at_z(sign * i))
 
     def g_relay():
         for way, sign in signs:
@@ -299,7 +320,7 @@
             g2_out[out, :] = total.astype(BF16)
             half_rows = pl.ds((way * 2 + way) * blk, blk)
             g2_out[half_rows, :] = (total[way * blk:(way + 1) * blk] + g1_in[last, :].astype(F32)).astype(BF16)
-            send(("g2", way, reach), g2_out.at[out], g2_in.at[there], at_z(sign * reach), "busy")
+            send(("g2", way, reach), g2_out.at[out], g2_in.at[there], at_z(sign * reach))
 
     def g_end():
         total = gn[tok(mid, n=2), :]
@@ -308,11 +329,29 @@
                 arrived(("g2", way, i), g2_in.at[g_rows(way, i)])
                 total = total + g2_in[g_rows(way, i), :].astype(F32)
         g_out[...] = total.astype(BF16)
-        send(("gx",), g_out.at[pl.ds(blk, blk), pl.ds(0, f)], gx_in, x_hi_peer, "busy")
-        send(("gl",), g_out.at[pl.ds(0, blk), pl.ds(f, f)], gl_in, x_lo_peer, "busy")
-        send(("gd",), g_out.at[pl.ds(blk, blk), pl.ds(f, f)], gd_in, x_both_peer, "busy")
+        first, second = pl.ds(0, blk), pl.ds(blk, blk)
+
+        @pl.when(busy)
+        def _():
+            gn[pl.ds(0, blk), :] = total[:blk]
+            send(("gx",), g_out.at[second], gx_in, x_hi_peer, "busy")
+
+        @pl.when(idle)
+        def _():
+            send(("gx",), g_out.at[second], gx_in, cross_both, "idle")
+            send(("gl",), g_out.at[first], gl_in, cross_lo, "idle")
+
+    def g_result():
         arrived(("gx",), gx_in)
-        o_normed[...] = (total[:blk, :f] + gx_in[...].astype(F32)).astype(BF16)
+
+        @pl.when(busy)
+        def _():
+            o_normed[...] = (gn[pl.ds(0, blk), :] + gx_in[...].astype(F32)).astype(BF16)
+
+        @pl.when(idle)
+        def _():
+            arrived(("gl",), gl_in)
+            o_normed[...] = (gl_in[...].astype(F32) + gx_in[...].astype(F32)).astype(BF16)
 
     down_rows = (((0,), (0,)), ((), ()))
 
@@ -344,35 +383,21 @@
     arrived(("wo",), w_out2)
     products()
     c_first()
+    turned_in[:, :f] = w_in[...].T
+    turned_in[:, f:] = w_in2[...].T
     c_relay()
     act()
-    e_relay()
-    e_end()
-    input_grad()
-
-    @pl.when(busy)
-    def _():
-        g_first()
-        g_send()
-
+    gather_and_grad()
+    g_send()
     other_weight_grads()
-
-    @pl.when(busy)
-    def _():
-        g_relay()
-
+    g_relay()
     weight_grads()
+    g_end()
     weight_grads_end()
-
-    @pl.when(busy)
-    def _():
-        g_end()
+    g_result()
 
     @pl.when(idle)
     def _():
-        arrived(("gl",), gl_in)
-        arrived(("gd",), gd_in)
-        o_normed[...] = (gl_in[...].astype(F32) + gd_in[...].astype(F32)).astype(BF16)
         for key, src in sent["idle"]:
             handle(key, src).wait_send()
 
@@ -411,6 +436,7 @@
             pltpu.VMEM((f, f), BF16),
             pltpu.VMEM((f, f), BF16),
             pltpu.VMEM((f, f), BF16),
+            pltpu.VMEM((f, 2 * f), BF16),
             pltpu.VMEM((rows, 4 * f), BF16),
             pltpu.VMEM((blk, 2 * f), BF16),
             pltpu.VMEM((rows, 2 * f), BF16),
@@ -418,15 +444,14 @@
             pltpu.VMEM((half * share, 2 * f), BF16),
             pltpu.VMEM((2 * share, 2 * f), BF16),
             pltpu.VMEM((half * share, 2 * f), BF16),
-            pltpu.VMEM((rows, 2 * f), F32),
-            pltpu.VMEM((rows, 2 * f), BF16),
-            pltpu.VMEM((rows, 2 * f), BF16),
-            pltpu.VMEM((rows, 2 * f), BF16),
-            pltpu.VMEM((2 * reach * 2 * blk, 2 * f), BF16),
-            pltpu.VMEM((2 * 2 * blk, 2 * f), BF16),
-            pltpu.VMEM((2 * reach * 2 * blk, 2 * f), BF16),
-            pltpu.VMEM((2 * blk, 2 * f), BF16),
-            pltpu.VMEM((blk, f), BF16),
+            pltpu.VMEM((rows, f), F32),
+            pltpu.VMEM((rows, f), BF16),
+            pltpu.VMEM((rows, f), BF16),
+            pltpu.VMEM((rows, f), BF16),
+            pltpu.VMEM((2 * reach * 2 * blk, f), BF16),
+            pltpu.VMEM((2 * 2 * blk, f), BF16),
+            pltpu.VMEM((2 * reach * 2 * blk, f), BF16),
+            pltpu.VMEM((2 * blk, f), BF16),
             pltpu.VMEM((blk, f), BF16),
             pltpu.VMEM((blk, f), BF16),
             pltpu.VMEM((f, f), BF16),
@@ -440,9 +465,10 @@
             pltpu.SemaphoreType.DMA((n,)),
         ],
         compiler_params=pltpu.CompilerParams(
-            collective_id=0, has_side_effects=True, vmem_limit_bytes=60 * 2**20),
+            collective_id=0, has_side_effects=True, vmem_limit_bytes=32 * 2**20),
         name="mlp_backward",
-    )(normed, upstream, loss_weight.reshape(1, blk), w_in, b_in, w_out)
+    )(*[pltpu.with_memory_space_constraint(x, pltpu.HBM) for x in (
+        normed, upstream, loss_weight.reshape(1, blk), w_in, b_in, w_out)])
     return outs[0], outs[1], outs[2], outs[3]
 
 

time: 95.7 us -> 90.9 us (0.950)
  the two profiles are of different devices: /device:TPU:8 before, /device:TPU:1 now
where the time goes in v3:
time: 90.9 us; the launch traced here: 90.7 us
  Pallas kernels  87.3 us (96%)
  local copies, waits for them, and re-layouts  2.81 us (3%)
    pallas_call x1, Pallas kernels, on_device(): pl.pallas_call(functools.partial(kernel, ny, nz, blk, f), out_shape=(jax....  87.3 us
    unnamed x4, local copies, waits for them, and re-layouts  2.81 us

profile of v3, /device:TPU:1, one launch (start us, length us, event | category | flops | bytes accessed | tf_op | source)
XLA Modules:
  0.0 90.7 jit_solution(9882283729745300237)
XLA Ops:
  0.6 87.3 %mlp_backward.1 = (bf16[16,384]{1,0:T(8,128)(2,1)S(1)}, f32[384,384]{1,0:T(8,128)S(1)}, f32[384]{0:T(512)S(1)}, f32[384,384]{1,0:T(8,128)S(1)}) custom-call(bf16[16,384]{1,0:T(8,128)(2,1)} %normed_hbm.1, bf16[16,384]{1,0:T(8,128)(2,1)} %upstream_hbm.1, f32[1,16]{1,0:T(1,128)} %bitcast.1, bf16[384,384]{1,0:T(8,128)(2,1)} %w_in_hbm.1, f32[384]{0:T(512)} %b_in_hbm.1, ...), custom_call_target="tpu_custom_call" | custom-call | tf_op jit(solution)/shard_map/mlp_backward/pallas_call | solution.py:420
  87.9 0.6 copy.14
  88.5 0.8 copy.15
  89.3 0.6 copy.16
  89.9 0.8 copy.17

commit v4 on v3

--- a/solution.py
+++ b/solution.py
@@ -69,6 +69,21 @@
             src_ref=ref, dst_ref=ref, send_sem=send_sem.at[ids[key]], recv_sem=recv_sem.at[ids[key]],
             device_id=sibling, device_id_type=MESH)
 
+    def flush(who, kept=()):
+        for key, src in sent[who]:
+            if key[0] not in kept:
+                handle(key, src).wait_send()
+        sent[who][:] = [(key, src) for key, src in sent[who] if key[0] in kept]
+
+    def flush_both():
+        @pl.when(busy)
+        def _():
+            flush("busy")
+
+        @pl.when(idle)
+        def _():
+            flush("idle")
+
     def arrived(key, dst):
         handle(key, dst).wait_recv()
 
@@ -177,13 +192,14 @@
             rows = tok(spans[i][0], n=2 * spans[i][1])
             arrived(("as", i), hg.at[rows])
 
-    def products():
-        part[:, :f] = (jnp.dot(hg[:, :f], w_in[...], preferred_element_type=F32)
-                       + jnp.dot(hg[:, 2 * f:3 * f], w_in2[...], preferred_element_type=F32)).astype(BF16)
+    def products(d):
+        rows = owned(d)
+        part[rows, :f] = (jnp.dot(hg[rows, :f], w_in[...], preferred_element_type=F32)
+                          + jnp.dot(hg[rows, 2 * f:3 * f], w_in2[...], preferred_element_type=F32)).astype(BF16)
         turned = (((1,), (1,)), ((), ()))
-        part[:, f:] = (
-            lax.dot_general(hg[:, f:2 * f], w_out[...], turned, preferred_element_type=F32)
-            + lax.dot_general(hg[:, 3 * f:], w_out2[...], turned, preferred_element_type=F32)).astype(BF16)
+        part[rows, f:] = (
+            lax.dot_general(hg[rows, f:2 * f], w_out[...], turned, preferred_element_type=F32)
+            + lax.dot_general(hg[rows, 3 * f:], w_out2[...], turned, preferred_element_type=F32)).astype(BF16)
 
     share = 2 * nz * blk // ny
 
@@ -201,9 +217,12 @@
         for i in range(hop, 0, -1):
             for way, sign in signs:
                 j = way if i == hop else None
+                if i < hop or way == 0:
+                    products(sign * (hop + i))
                 send(("c1", way, i), part.at[owned(sign * (hop + i), j)], c1_in.at[stage(way, i, j)], at_y(sign * i))
         for i in range(hop - 1, 0, -1):
             for way, sign in signs:
+                products(sign * i)
                 send(("c2", way, i), part.at[owned(sign * i)], c2_in.at[stage(way, i)], at_y(sign * i))
 
     def c_relay():
@@ -381,10 +400,12 @@
         load.wait()
     arrived(("wi",), w_in2)
     arrived(("wo",), w_out2)
-    products()
     c_first()
+    for d in (hop, -hop, 0):
+        products(d)
     turned_in[:, :f] = w_in[...].T
     turned_in[:, f:] = w_in2[...].T
+    flush_both()
     c_relay()
     act()
     gather_and_grad()
@@ -392,22 +413,13 @@
     other_weight_grads()
     g_relay()
     weight_grads()
+    flush("all", ("vo", "vi", "vb"))
     g_end()
     weight_grads_end()
     g_result()
 
-    @pl.when(idle)
-    def _():
-        for key, src in sent["idle"]:
-            handle(key, src).wait_send()
-
-    @pl.when(busy)
-    def _():
-        for key, src in sent["busy"]:
-            handle(key, src).wait_send()
-
-    for key, src in sent["all"]:
-        handle(key, src).wait_send()
+    flush_both()
+    flush("all")
 
 
 def on_device(ny, nz, normed, upstream, loss_weight, w_in, b_in, w_out):

time: 90.9 us -> 90.6 us (level)
  no operation moved by 1% of the time
where the time goes in v4:
time: 90.6 us; the launch traced here: 90.4 us
  Pallas kernels  87 us (96%)
  local copies, waits for them, and re-layouts  2.81 us (3%)
    pallas_call x1, Pallas kernels, on_device(): pl.pallas_call(functools.partial(kernel, ny, nz, blk, f), out_shape=(jax....  87 us
    unnamed x4, local copies, waits for them, and re-layouts  2.81 us

profile of v4, /device:TPU:1, one launch (start us, length us, event | category | flops | bytes accessed | tf_op | source)
XLA Modules:
  0.0 90.4 jit_solution(2465649974944403740)
XLA Ops:
  0.6 87.0 %mlp_backward.1 = (bf16[16,384]{1,0:T(8,128)(2,1)S(1)}, f32[384,384]{1,0:T(8,128)S(1)}, f32[384]{0:T(512)S(1)}, f32[384,384]{1,0:T(8,128)S(1)}) custom-call(bf16[16,384]{1,0:T(8,128)(2,1)} %normed_hbm.1, bf16[16,384]{1,0:T(8,128)(2,1)} %upstream_hbm.1, f32[1,16]{1,0:T(1,128)} %bitcast.1, bf16[384,384]{1,0:T(8,128)(2,1)} %w_in_hbm.1, f32[384]{0:T(512)} %b_in_hbm.1, ...), custom_call_target="tpu_custom_call" | custom-call | tf_op jit(solution)/shard_map/mlp_backward/pallas_call | solution.py:432
  87.6 0.6 copy.14
  88.2 0.8 copy.15
  89.0 0.6 copy.16
  89.6 0.8 copy.17

commit v5 on v4

--- a/solution.py
+++ b/solution.py
@@ -401,12 +401,13 @@
     arrived(("wi",), w_in2)
     arrived(("wo",), w_out2)
     c_first()
-    for d in (hop, -hop, 0):
+    for d in (hop, -hop):
         products(d)
+    c_relay()
+    products(0)
     turned_in[:, :f] = w_in[...].T
     turned_in[:, f:] = w_in2[...].T
     flush_both()
-    c_relay()
     act()
     gather_and_grad()
     g_send()

time: 90.6 us -> 90 us (level)
  no operation moved by 1% of the time
where the time goes in v5:
time: 90 us; the launch traced here: 89.6 us
  Pallas kernels  86.1 us (96%)
  local copies, waits for them, and re-layouts  2.81 us (3%)
    pallas_call x1, Pallas kernels, on_device(): pl.pallas_call(functools.partial(kernel, ny, nz, blk, f), out_shape=(jax....  86.1 us
    unnamed x4, local copies, waits for them, and re-layouts  2.81 us

profile of v5, /device:TPU:1, one launch (start us, length us, event | category | flops | bytes accessed | tf_op | source)
XLA Modules:
  0.0 89.6 jit_solution(15145231251681410692)
XLA Ops:
  0.6 86.1 %mlp_backward.1 = (bf16[16,384]{1,0:T(8,128)(2,1)S(1)}, f32[384,384]{1,0:T(8,128)S(1)}, f32[384]{0:T(512)S(1)}, f32[384,384]{1,0:T(8,128)S(1)}) custom-call(bf16[16,384]{1,0:T(8,128)(2,1)} %normed_hbm.1, bf16[16,384]{1,0:T(8,128)(2,1)} %upstream_hbm.1, f32[1,16]{1,0:T(1,128)} %bitcast.1, bf16[384,384]{1,0:T(8,128)(2,1)} %w_in_hbm.1, f32[384]{0:T(512)} %b_in_hbm.1, ...), custom_call_target="tpu_custom_call" | custom-call | tf_op jit(solution)/shard_map/mlp_backward/pallas_call | solution.py:433
  86.8 0.6 copy.14
  87.4 0.8 copy.15
  88.2 0.6 copy.16
  88.8 0.8 copy.17
